TPU v7x, 256 devices: a whole 4x4x8 slice. The times are simulated.
256 devices in a mesh: dp: 32 (over y, x, core), mp: 8 (over z).
Axes of the slice: x: 4, y: 4, z: 8, core: 2. Of those that a mesh axis runs over, the one named last changes fastest.
Arguments:
- hidden: bfloat16 [16384, 18432], P('dp', 'mp'), may hold values from -6 to 6
- upstream: bfloat16 [16384, 2304], P('dp', 'mp'), may hold values from -1.5 to 1.5
- reward_head: float32 [2304], P('mp'), may hold values from -6 to 6
- margins: float32 [512], P('dp'), may hold values from -8 to 8
- ends: int32 [512, 2], P('dp'), may hold values from 0 to 511
- residual_error: bfloat16 [32, 18432, 2304], P('dp', 'mp'), may hold values from -24 to 24
- previous_q: float32 [2304, 32], replicated, may hold values from -6 to 6
Outputs:
- basis: float32 [18432, 32], P('mp')
- projection: float32 [2304, 32], replicated
All inputs are finite; a program needn't handle non-finite values.
Results may differ from a plain program's by a relative error of at most 0.0017.
Values may be sent and summed in bfloat16 or wider, within the bound.
A program may use at most 128 MiB of HBM per device.

v0:
```python
import math

import jax
import jax.numpy as jnp
from jax import lax
from jax.sharding import PartitionSpec as P

FF = 18432


HI = lax.Precision.HIGHEST
LEFT_T = (((0,), (0,)), ((), ()))


def orthonormal(factor):
    local_gram = lax.dot_general(factor, factor, LEFT_T, precision=HI)
    gram = lax.psum(local_gram, "mp")
    lower = jnp.linalg.cholesky(gram)
    return lax.linalg.triangular_solve(lower, factor, left_side=False, lower=True, transpose_a=True)


def combine_terms(share):
    return lax.psum(share, ("dp", "mp"))


def shards(hidden, upstream, reward_head, margins, ends, residual_error, previous_q):
    tok_rows, local_width = upstream.shape
    push = jax.nn.sigmoid(-margins)
    pair_coef = jnp.stack([-push, push], axis=1).reshape(-1)
    spots = ends.reshape(-1)
    places = jnp.arange(tok_rows, dtype=jnp.int32)
    marks = (spots[:, None] == places[None, :]).astype(jnp.float32)
    token_weight = jnp.dot(pair_coef, marks, precision=HI)
    cotangent = (
        upstream.astype(jnp.float32) + token_weight[:, None] * reward_head[None, :]
    ).astype(jnp.bfloat16)
    error = residual_error[0]
    block = lax.dot_general(
        hidden,
        lax.all_gather(cotangent, "mp", axis=1, tiled=True),
        LEFT_T,
        preferred_element_type=jnp.float32,
    )
    gradient = block + error.astype(jnp.float32)
    factor = lax.psum(jnp.dot(gradient, previous_q, precision=HI), "dp")
    ortho = orthonormal(factor)
    share = lax.dot_general(gradient, ortho, LEFT_T, precision=HI)
    projection = combine_terms(share) / lax.axis_size("dp")
    return (ortho * math.sqrt(FF), projection)


def solution(mesh):
    in_specs = (
        P("dp", "mp"),
        P("dp", "mp"),
        P("mp"),
        P("dp"),
        P("dp", None),
        P("dp", "mp", None),
        P(),
    )
    out_specs = (P("mp", None), P())
    return jax.shard_map(shards, mesh=mesh, in_specs=in_specs, out_specs=out_specs, check_vma=False)
```

profile of v0, /device:TPU:1, one launch (start us, length us, event | category | flops | bytes accessed | tf_op | source)
XLA Modules:
  0.0 509.5 jit_solution(2501106987979844803)
XLA Ops:
  7.2 0.0 copy-start
  7.2 0.0 all-gather.2.cloned.1.call-start
  7.2 0.8 negate_bitcast_fusion
  8.1 0.1 copy.14
  8.1 0.1 reshape.23
  8.2 0.8 copy.15
  9.0 0.1 eq.15
  9.1 0.2 fusion
  9.3 1.8 add_convert_fusion
  11.1 0.0 all-gather.2.cloned.1.call-update
  11.1 0.0 all-reduce.3.cloned.1.call-start
  11.2 14.6 %copy.16 = bf16[1,2304,2304]{1,2,0:T(8,128)(2,1)} copy(bf16[1,2304,2304]{2,1,0:T(8,128)(2,1)} %param.12) | data formatting | bytes 21233664 | tf_op args[5]
  25.7 0.0 copy-start.1
  25.7 28.0 %all-gather.2.cloned.1.call-done = bf16[512,2304]{0,1:T(8,128)(2,1)} async-done(((bf16[512,288]{0,1:T(8,128)(2,1)}), bf16[512,2304]{0,1:T(8,128)(2,1)}) %all-gather.2.cloned.1.call-update) | async-done | bytes 2359312 | tf_op jit(solution)/shard_map/all_gather | solution.py:40
  53.7 0.0 copy-done
  53.7 14.4 %convert_add_fusion = f32[2304,2304]{0,1:T(8,128)} fusion(bf16[512,2304]{0,1:T(8,128)(2,1)} %all-gather.2.cloned.1.call-done, bf16[512,2304]{1,0:T(8,128)(2,1)S(1)} %copy-done, bf16[1,2304,2304]{1,2,0:T(8,128)(2,1)} %copy.16), kind=kOutput, calls=%fused_computation | convolution fusion | flops 5446434816 | bytes 36569088 | tf_op jit(solution)/shard_map/dot_general | solution.py:38
  68.1 0.0 copy-done.1
  68.1 15.9 %fusion.6 = f32[2304,32]{0,1:T(8,128)} fusion(f32[2304,2304]{0,1:T(8,128)} %convert_add_fusion, f32[2304,32]{0,1:T(8,128)S(1)} %copy-done.1), kind=kOutput, calls=%fused_computation.20 | convolution fusion | flops 2038431744 | bytes 21823488 | tf_op jit(solution)/shard_map/dot_general | solution.py:45
  84.0 0.0 all-reduce.3.cloned.1.call-update
  84.0 0.0 all-reduce.5.cloned.1.call-start
  84.1 112.4 %all-reduce.3.cloned.1.call-done = f32[2304,32]{0,1:T(8,128)} async-done(((f32[2304,32]{0,1:T(8,128)}), f32[2304,32]{0,1:T(8,128)}) %all-reduce.3.cloned.1.call-update) | async-done | bytes 294928 | tf_op jit(solution)/shard_map/psum | solution.py:45
  196.4 1.4 fusion.7
  197.9 23.0 %psum.22 = f32[32,32]{0,1:T(8,128)S(1)} all-reduce(f32[32,32]{0,1:T(8,128)S(1)} %fusion.7), channel_id=1, replica_groups=mesh['dp'=32,'mp'=8] {'mp'}, use_global_device_ids=true, to_apply=%region_1.0 | all-reduce | flops 1024 | bytes 8192 | tf_op jit(solution)/shard_map/psum | solution.py:17
  220.9 0.1 copy.18
  221.0 2.9 cholesky.16
  223.9 0.6 compare_reduce_fusion
  224.6 0.7 fusion.2
  225.2 2.4 custom-call.6
  227.7 2.1 broadcast_multiply_fusion.1
  229.8 23.2 %fusion.8 = f32[2304,32]{0,1:T(8,128)} fusion(f32[2304,2304]{0,1:T(8,128)} %convert_add_fusion, f32[2304,32]{0,1:T(8,128)S(1)} %get-tuple-element.5), kind=kOutput, calls=%fused_computation.22 | convolution fusion | flops 2038431744 | bytes 21823488 | tf_op jit(solution)/shard_map/dot_general | solution.py:47
  253.0 0.0 all-reduce.5.cloned.1.call-update
  253.0 248.3 %all-reduce.5.cloned.1.call-done = f32[2304,32]{0,1:T(8,128)} async-done(((f32[2304,32]{0,1:T(8,128)}), f32[2304,32]{0,1:T(8,128)}) %all-reduce.5.cloned.1.call-update) | async-done | bytes 294928 | tf_op jit(solution)/shard_map/psum | solution.py:23
  501.3 1.7 broadcast_multiply_fusion
  (3 shorter events, 0.0 us)
Async XLA Ops:
  7.2 46.6 %copy-start = (bf16[512,2304]{1,0:T(8,128)(2,1)S(1)}, bf16[512,2304]{1,0:T(8,128)(2,1)}, u32[]{:S(2)}) copy-start(bf16[512,2304]{1,0:T(8,128)(2,1)} %param.7) | copy-start | bytes 7077892
  7.2 46.5 %all-gather.2.cloned.1.call-start = ((), (), s32[]{:S(2)}) async-start(), calls=%async_computation | async-start | bytes 2654208 | tf_op jit(solution)/shard_map/all_gather | solution.py:40
  11.1 185.3 %all-reduce.3.cloned.1.call-start = ((), (), s32[]{:S(2)}) async-start(), calls=%async_computation.1 | async-start | bytes 589824 | tf_op jit(solution)/shard_map/psum | solution.py:45
  25.7 42.4 %copy-start.1 = (f32[2304,32]{0,1:T(8,128)S(1)}, f32[2304,32]{0,1:T(8,128)}, u32[]{:S(2)}) copy-start(f32[2304,32]{0,1:T(8,128)} %param.13) | copy-start | bytes 884740
  84.0 417.3 %all-reduce.5.cloned.1.call-start = ((), (), s32[]{:S(2)}) async-start(), calls=%async_computation.2 | async-start | bytes 589824 | tf_op jit(solution)/shard_map/psum | solution.py:23
Sparse Core Ops, SparseCore 0:
  11.3 42.4 all-gather.1
  84.1 112.2 all-reduce.2
  253.1 248.1 all-reduce.4
where the time goes:
time: 510 us
  waiting for transfers between devices  389 us (76%)
  matrix products  57.2 us (11%)
  blocking collectives  23 us (5%)
  local copies, waits for them, and re-layouts  15.7 us (3%)
  between operations  13.8 us (3%)
  other arithmetic  11 us (2%)
    psum x1, waiting for transfers between devices, combine_terms(): return lax.psum(share, ('dp', 'mp'))  248 us
    psum x1, waiting for transfers between devices, shards(): factor = lax.psum(jnp.dot(gradient, previous_q, precision=HI), 'dp')  112 us
    all_gather x1, waiting for transfers between devices, shards(): lax.all_gather(cotangent, 'mp', axis=1, tiled=True)  28 us
    dot_general x1, matrix products, shards(): share = lax.dot_general(gradient, ortho, LEFT_T, precision=HI)  23.2 us
    psum x1, blocking collectives, orthonormal(): gram = lax.psum(local_gram, 'mp')  23 us
    dot_general x1, matrix products, shards(): factor = lax.psum(jnp.dot(gradient, previous_q, precision=HI), 'dp')  15.9 us
    unnamed x6, local copies, waits for them, and re-layouts  15.3 us
    dot_general x1, matrix products, shards(): lax.dot_general(hidden, lax.all_gather(cotangent, 'mp', axis=1, tiled=Tru...  14.4 us
  transfers between devices with their start and end apart: 3, of which 3 were waited for; matrix products, arithmetic and copies ran while one was open for 3% of the time, Pallas kernels for 0%

commit v1 on v0

v1 whole, which is shorter than its diff:
```python
import math

import jax
import jax.numpy as jnp
from jax import lax
from jax.experimental import pallas as pl
from jax.experimental.pallas import tpu as pltpu
from jax.sharding import PartitionSpec as P

FF = 18432
D = 2304
RANK = 32
TOK = 512
PAIRS = 16
WIDTH = 288
Z = 8
NDP = 32
OWNERS = 24
CH = 384
PARTS = 9
PART = D // PARTS
MESH = pl.DeviceIdType.MESH
HI = lax.Precision.HIGHEST
F32 = jnp.float32
BF16 = jnp.bfloat16


def ring(step, size):
    return min(step, size - step)


PLANE = sorted(
    ((dy, dx, dc) for dy in range(4) for dx in range(4) for dc in range(2) if (dy, dx, dc) != (0, 0, 0)),
    key=lambda o: -(ring(o[0], 4) + ring(o[1], 4)),
)
LINE = (4, 3, 5, 2, 6, 1, 7)


def split(x):
    high = x.astype(BF16)
    low = (x - high.astype(F32)).astype(BF16)
    return jnp.concatenate([high, low], axis=0)


def fold(x):
    half = x.shape[0] // 2
    return x[:half] + x[half:]


def mm(a, b):
    return lax.dot_general(a, b, (((1,), (0,)), ((), ())), preferred_element_type=F32)


def mm_t(a, b):
    return lax.dot_general(a, b, (((1,), (1,)), ((), ())), preferred_element_type=F32)


def column(row):
    n = row.shape[1]
    same = lax.broadcasted_iota(jnp.int32, (n, n), 0) == lax.broadcasted_iota(jnp.int32, (n, n), 1)
    return jnp.sum(jnp.where(same, jnp.broadcast_to(row, (n, n)), 0.0), axis=1, keepdims=True)


def inverse_lower(gram):
    rows = lax.broadcasted_iota(jnp.int32, (RANK, 128), 0)
    lanes = lax.broadcasted_iota(jnp.int32, (RANK, 128), 1)
    eye = (lanes == rows + RANK).astype(F32)
    m = jnp.concatenate([gram, jnp.zeros((RANK, 128 - RANK), F32)], axis=1) + eye
    for k in range(RANK - 1):
        col = m[:, k : k + 1]
        pivot = m[k : k + 1, :]
        scale = jnp.where(rows[:, :1] > k, col / m[k : k + 1, k : k + 1], 0.0)
        m = m - scale * pivot
    diag = jnp.sum(jnp.where(lanes == rows, m, 0.0), axis=1, keepdims=True)
    return (m * lax.rsqrt(diag))[:, RANK : 2 * RANK]


def kernel(
    hidden, upstream_t, head, margins, ends_t, error, q_t,
    basis_out, proj_out,
    h, e, u, hd, mg, en, q, q2, cot, c128,
    p_part, p_in, p_red, p_full,
    f_part, f_in, f_red, f_full,
    w_part, w_in, g_part, g_in,
    s_part, s_in, s_red, z_in, s_tot, s_full, b_out, r_out,
    load, e_load, out_sem,
    p_s, p_r, pg_s, pg_r, c_s, c_r, f_s, f_r, fg_s, fg_r,
    w_s, w_r, g_s, g_r, s_s, s_r, zs_s, zs_r, sg_s, sg_r,
):
    dp, z = lax.axis_index("dp"), lax.axis_index("mp")
    core, chip = lax.rem(dp, 2), lax.div(dp, 2)
    cy, cx = lax.div(chip, 4), lax.rem(chip, 4)

    def owns(y, x, c):
        return jnp.logical_or(c == 0, lax.rem(x + y, 2) == 0)

    def owned(y, x, c):
        place = y * 4 + x
        return jnp.where(c == 0, place, 16 + lax.div(place, 2))

    def chunk(ref, k):
        row = pl.multiple_of(lax.div(k, 6) * 8, 8)
        lane = pl.multiple_of(lax.rem(k, 6) * CH, 128)
        return ref.at[pl.ds(row, 8), pl.ds(lane, CH)]

    def away(o):
        dy, dx, dc = o
        return lax.rem(cy + dy, 4), lax.rem(cx + dx, 4), lax.rem(core + dc, 2)

    def along(step):
        return lax.rem(z + step, Z)

    is_owner, mine = owns(cy, cx, core), owned(cy, cx, core)

    def remote(src, dst, send, recv, **to):
        return pltpu.make_async_remote_copy(
            src_ref=src, dst_ref=dst, send_sem=send, recv_sem=recv, device_id=to, device_id_type=MESH
        )

    def arrived(ref, sem):
        pltpu.make_async_copy(ref, ref, sem).wait()

    loads = [
        pltpu.make_async_copy(src, dst, load.at[i])
        for i, (src, dst) in enumerate(
            [(upstream_t, u), (margins, mg), (ends_t, en), (head, hd), (q_t, q), (hidden, h)]
        )
    ]
    e_loads = [
        pltpu.make_async_copy(error.at[0, pl.ds(PART * i, PART)], e.at[pl.ds(PART * i, PART)], e_load.at[i])
        for i in range(PARTS)
    ]
    for c in loads[:5] + e_loads + loads[5:]:
        c.start()

    barrier = pltpu.get_barrier_semaphore()
    for o in PLANE:
        y, x, c = away(o)
        pl.semaphore_signal(barrier, inc=1, device_id={"dp": (y * 4 + x) * 2 + c}, device_id_type=MESH)
    for step in LINE:
        pl.semaphore_signal(barrier, inc=1, device_id={"mp": along(step)}, device_id_type=MESH)

    shift = pl.multiple_of(lax.rem(z, 4) * 32, 32)
    window = pl.multiple_of((2 * z + lax.div(z, 4)) * 128, 128)
    cot[...] = jnp.zeros_like(cot)
    for c in loads[:5]:
        c.wait()
    push = jax.nn.sigmoid(-column(mg[...]))
    spots = en[...].astype(F32)
    places = lax.broadcasted_iota(jnp.int32, (PAIRS, TOK), 1).astype(F32)
    weight = jnp.sum(
        jnp.where(places == column(spots[1:2]), push, 0.0) - jnp.where(places == column(spots[0:1]), push, 0.0),
        axis=0,
        keepdims=True,
    )
    direction = jnp.broadcast_to(hd[...], (128, WIDTH)).T[:, :1]
    cot[pl.ds(shift, WIDTH), :] = (u[...].astype(F32) + direction * weight).astype(BF16)
    q2[...] = split(q[...])
    p_part[...] = fold(mm(q2[:, pl.ds(window, CH)], cot[...]))
    pl.semaphore_wait(barrier, NDP - 1 + Z - 1)

    def p_chunk(ref, t):
        row = pl.multiple_of(lax.div(t, 2) * 8, 8)
        return ref.at[pl.ds(row, 8), pl.ds(pl.multiple_of(lax.rem(t, 2) * 256, 128), 256)]

    p_sends = [
        remote(p_chunk(p_part, along(o)), p_in.at[j], p_s.at[j], p_r, mp=along(o)) for j, o in enumerate(LINE)
    ]
    for c in p_sends:
        c.start()
    for i in range(PARTS):
        e_loads[i].wait()
        f_part[:, PART * i : PART * (i + 1)] = fold(mm_t(q2[...], e[PART * i : PART * (i + 1), :]))
    loads[5].wait()
    arrived(p_in, p_r)
    total = p_chunk(p_part, z)[...]
    for j in range(Z - 1):
        total += p_in[j]
    p_red[...] = total
    pg_sends = [remote(p_red, p_chunk(p_full, z), pg_s.at[j], pg_r, mp=along(o)) for j, o in enumerate(LINE)]
    for c in pg_sends:
        c.start()
    pltpu.make_async_copy(p_red, p_chunk(p_full, z), pg_r).start()

    def c_rows(ref):
        return ref.at[pl.ds(pl.multiple_of(z * WIDTH, 32), WIDTH)]

    def c_lanes(t):
        lane = pl.multiple_of(lax.div(t, 2) * 128, 128)
        return cot.at[pl.ds(shift, WIDTH), pl.ds(lane, 128)]

    c_sends = [
        remote(c_lanes(along(o)), c_rows(c128), c_s.at[j], c_r, mp=along(o)) for j, o in enumerate(LINE)
    ]
    for c in c_sends:
        c.start()
    pltpu.make_async_copy(c_lanes(z), c_rows(c128), c_r).start()
    for c in p_sends:
        c.wait_send()
    arrived(p_full, pg_r)
    f_part[...] += fold(mm(split(p_full[...]), h[...]))

    def to_owners(part, into, send, recv, start):
        for j, o in enumerate(PLANE):
            y, x, c = away(o)

            @pl.when(owns(y, x, c))
            def _(j=j, y=y, x=x, c=c):
                copy = remote(
                    chunk(part, owned(y, x, c)), into.at[j], send.at[j], recv, dp=(y * 4 + x) * 2 + c
                )
                if start:
                    copy.start()
                else:
                    copy.wait_send()

    def add_up(part, into, recv):
        arrived(into, recv)
        total = chunk(part, mine)[...]
        for j in range(NDP - 1):
            total += into[j]
        return total

    def hand_round(red, full, send, recv, start):
        for j, o in enumerate(PLANE):
            y, x, c = away(o)
            copy = remote(red, chunk(full, mine), send.at[j], recv, dp=(y * 4 + x) * 2 + c)
            if start:
                copy.start()
            else:
                copy.wait_send()

    to_owners(f_part, f_in, f_s, f_r, True)
    for c in pg_sends + c_sends:
        c.wait_send()

    @pl.when(is_owner)
    def _():
        f_red[...] = add_up(f_part, f_in, f_r)
        hand_round(f_red, f_full, fg_s, fg_r, True)
        pltpu.make_async_copy(f_red, chunk(f_full, mine), fg_r).start()

    to_owners(f_part, f_in, f_s, f_r, False)
    arrived(c128, c_r)
    arrived(f_full, fg_r)

    f2 = split(f_full[...])
    w_part[...] = fold(mm_t(f2, h[...]))

    def w_chunk(ref, t):
        row = pl.multiple_of(lax.rem(t, 2) * 16, 16)
        return ref.at[pl.ds(row, 16), pl.ds(pl.multiple_of(lax.div(t, 2) * 128, 128), 128)]

    w_sends = [
        remote(w_chunk(w_part, along(o)), w_in.at[j], w_s.at[j], w_r, mp=along(o)) for j, o in enumerate(LINE)
    ]
    for c in w_sends:
        c.start()
    gram = mm_t(f2, f2)
    g_part[...] = fold(gram[:, :RANK] + gram[:, RANK:])
    g_sends = [remote(g_part, g_in.at[z], g_s.at[j], g_r, mp=along(o)) for j, o in enumerate(LINE)]
    for c in g_sends:
        c.start()
    pltpu.make_async_copy(g_part, g_in.at[z], g_r).start()

    s_part[...] = fold(mm(f2, e[...]))

    @pl.when(is_owner)
    def _():
        hand_round(f_red, f_full, fg_s, fg_r, False)

    for c in w_sends + g_sends:
        c.wait_send()
    arrived(w_in, w_r)
    total = w_chunk(w_part, z)[...]
    for j in range(Z - 1):
        total += w_in[j]
    half = pl.ds(pl.multiple_of(lax.rem(z, 2) * 16, 16), 16)
    s_part[half, :] += fold(mm_t(split(total), c128[...]))

    to_owners(s_part, s_in, s_s, s_r, True)
    arrived(g_in, g_r)
    total = g_in[0]
    for j in range(1, Z):
        total += g_in[j]
    inverse = inverse_lower(total)

    @pl.when(is_owner)
    def _():
        s_red[...] = add_up(s_part, s_in, s_r)
        for j, o in enumerate(LINE):
            remote(s_red, z_in.at[z], zs_s.at[j], zs_r, mp=along(o)).start()
        pltpu.make_async_copy(s_red, z_in.at[z], zs_r).start()

    b_out[...] = jnp.dot(inverse * math.sqrt(FF), f_full[...], precision=HI, preferred_element_type=F32)
    out = pltpu.make_async_copy(b_out, basis_out, out_sem.at[0])
    out.start()

    @pl.when(is_owner)
    def _():
        arrived(z_in, zs_r)
        total = z_in[0]
        for j in range(1, Z):
            total += z_in[j]
        s_tot[...] = total
        hand_round(s_tot, s_full, sg_s, sg_r, True)
        pltpu.make_async_copy(s_tot, chunk(s_full, mine), sg_r).start()
        for j, o in enumerate(LINE):
            remote(s_red, z_in.at[z], zs_s.at[j], zs_r, mp=along(o)).wait_send()

    to_owners(s_part, s_in, s_s, s_r, False)
    arrived(s_full, sg_r)
    r_out[...] = jnp.dot(inverse * (1.0 / NDP), s_full[...], precision=HI, preferred_element_type=F32)
    last = pltpu.make_async_copy(r_out, proj_out, out_sem.at[1])
    last.start()

    @pl.when(is_owner)
    def _():
        hand_round(s_tot, s_full, sg_s, sg_r, False)

    out.wait()
    last.wait()


def shards(hidden, upstream, reward_head, margins, ends, residual_error, previous_q):
    any_spec = pl.BlockSpec(memory_space=pl.ANY)
    vmem, dma = pltpu.VMEM, pltpu.SemaphoreType.DMA
    whole = jax.ShapeDtypeStruct((RANK, D), F32)
    line, plane, one = dma((Z - 1,)), dma((NDP - 1,)), dma(())
    basis, projection = pl.pallas_call(
        kernel,
        out_shape=(whole, whole),
        in_specs=[any_spec] * 7,
        out_specs=(any_spec, any_spec),
        scratch_shapes=[
            vmem((TOK, D), BF16), vmem((D, D), BF16), vmem((WIDTH, TOK), BF16), vmem((1, WIDTH), F32),
            vmem((1, PAIRS), F32), vmem((2, PAIRS), jnp.int32), vmem((RANK, D), F32), vmem((2 * RANK, D), BF16),
            vmem((CH, TOK), BF16), vmem((D, 128), BF16),
            vmem((RANK, TOK), F32), vmem((Z - 1, 8, 256), F32), vmem((8, 256), F32), vmem((RANK, TOK), F32),
            vmem((RANK, D), F32), vmem((NDP - 1, 8, CH), F32), vmem((8, CH), F32), vmem((RANK, D), F32),
            vmem((RANK, TOK), F32), vmem((Z - 1, 16, 128), F32),
            vmem((RANK, RANK), F32), vmem((Z, RANK, RANK), F32),
            vmem((RANK, D), F32), vmem((NDP - 1, 8, CH), F32), vmem((8, CH), F32), vmem((Z, 8, CH), F32),
            vmem((8, CH), F32), vmem((RANK, D), F32), vmem((RANK, D), F32), vmem((RANK, D), F32),
            dma((6,)), dma((PARTS,)), dma((2,)),
            line, one, line, one, line, one, plane, one, plane, one,
            line, one, line, one, plane, one, line, one, plane, one,
        ],
        compiler_params=pltpu.CompilerParams(
            collective_id=0, has_side_effects=True, vmem_limit_bytes=48 * 1024 * 1024
        ),
        cost_estimate=pl.CostEstimate(flops=2_000_000_000, bytes_accessed=14_000_000, transcendentals=0),
        name="power_step",
    )(
        hidden, upstream.T, reward_head.reshape(1, WIDTH), margins.reshape(1, PAIRS), ends.T, residual_error,
        previous_q.T,
    )
    return basis.T, projection.T


def solution(mesh):
    in_specs = (
        P("dp", "mp"),
        P("dp", "mp"),
        P("mp"),
        P("dp"),
        P("dp", None),
        P("dp", "mp", None),
        P(),
    )
    out_specs = (P("mp", None), P())
    return jax.shard_map(shards, mesh=mesh, in_specs=in_specs, out_specs=out_specs, check_vma=False)
```

time: 510 us -> 70.9 us (0.14)
  waiting for transfers between devices: 389 us -> 0 us
  Pallas kernels: 0 us -> 63 us
  matrix products: 57.2 us -> 0 us
  blocking collectives: 23 us -> 0 us
  between operations: 13.8 us -> 0.64 us
  other arithmetic: 11 us -> 0 us
  local copies, waits for them, and re-layouts: 15.7 us -> 7.03 us
    psum x2 -> x0, waiting for transfers between devices: 361 us -> none  [the longest x1 248 us: combine_terms(): return lax.psum(share, ('dp', 'mp'))]
    pallas_call x0 -> x1, Pallas kernels: none -> 63 us  [shards(): pl.pallas_call(kernel, out_shape=(whole, whole), in_specs=[any_spec] * 7,...]
    dot_general x5 -> x0, matrix products: 55.1 us -> none  [the longest x1 23.2 us: shards(): share = lax.dot_general(gradient, ortho, LEFT_T, precision=HI)]
    all_gather x1 -> x0, waiting for transfers between devices: 28 us -> none  [shards(): lax.all_gather(cotangent, 'mp', axis=1, tiled=True)]
    psum x1 -> x0, blocking collectives: 23 us -> none  [orthonormal(): gram = lax.psum(local_gram, 'mp')]
    unnamed x6 -> x12, local copies, waits for them, and re-layouts: 15.3 us -> 6.35 us
    another operation x7 -> x0, other arithmetic: 7.5 us -> none  [the longest x3 3.59 us: orthonormal(): lower = jnp.linalg.cholesky(gram)]
  transfers between devices with their start and end apart: 3 -> 0, of which waited for: 3 -> 0; matrix products, arithmetic and copies ran while one was open for 3% -> 0% of each run, Pallas kernels for 0% -> 0%
where the time goes in v1:
time: 70.9 us; the launch traced here: 70.6 us
  Pallas kernels  63 us (89%)
  local copies, waits for them, and re-layouts  7.03 us (10%)
    pallas_call x1, Pallas kernels, shards(): pl.pallas_call(kernel, out_shape=(whole, whole), in_specs=[any_spec] * 7,...  63 us
    unnamed x12, local copies, waits for them, and re-layouts  6.35 us

profile of v1, /device:TPU:1, one launch (start us, length us, event | category | flops | bytes accessed | tf_op | source)
XLA Modules:
  0.0 70.6 jit_solution(10914327923568597428)
XLA Ops:
  0.6 0.7 reshape.10.head
  1.3 0.0 copy-start
  1.3 1.7 %copy-done = bf16[512,2304]{1,0:T(8,128)(2,1)S(1)} copy-done((bf16[512,2304]{1,0:T(8,128)(2,1)S(1)}, bf16[512,2304]{1,0:T(8,128)(2,1)}, u32[]{:S(2)}) %copy-start) | copy-done | bytes 2359320
  3.0 0.0 copy-start.1
  3.0 1.0 %copy-done.1 = bf16[512,288]{0,1:T(8,128)(2,1)S(1)} copy-done((bf16[512,288]{0,1:T(8,128)(2,1)S(1)}, bf16[512,288]{0,1:T(8,128)(2,1)}, u32[]{:S(2)}) %copy-start.1) | copy-done | bytes 294936
  3.9 0.0 copy-start.2
  3.9 1.0 %copy-done.2 = f32[2304,32]{0,1:T(8,128)S(1)} copy-done((f32[2304,32]{0,1:T(8,128)S(1)}, f32[2304,32]{0,1:T(8,128)}, u32[]{:S(2)}) %copy-start.2) | copy-done | bytes 294936
  4.9 0.0 copy-start.3
  4.9 0.7 copy-done.3
  5.6 0.0 copy-start.4
  5.6 0.7 copy-done.4
  6.2 63.0 %power_step.1 = (f32[32,2304]{1,0:T(8,128)S(1)}, f32[32,2304]{1,0:T(8,128)S(1)}) custom-call(bf16[512,2304]{1,0:T(8,128)(2,1)S(1)} %copy-done, bf16[288,512]{1,0:T(8,128)(2,1)S(1)} %bitcast.6, f32[1,288]{1,0:T(1,128)S(1)} %reshape.10.head, f32[1,16]{1,0:T(1,128)S(1)} %bitcast.11, s32[2,16]{1,0:T(2,128)S(1)} %bitcast.10, bf16[1,2304,2304]{2,1,0:T(8,128)(2,1)} %error.1, ...), custom_call_target="tpu_custom_call" | custom-call | flops 2000000000 | bytes 14000000 | tf_op jit(solution)/shard_map/power_step/pallas_call | solution.py:330
  69.2 0.7 %copy.11 = f32[2304,32]{0,1:T(8,128)} copy(f32[2304,32]{0,1:T(8,128)S(1)} %bitcast.9) | data formatting | bytes 589824
  69.9 0.7 %copy.12 = f32[2304,32]{0,1:T(8,128)} copy(f32[2304,32]{0,1:T(8,128)S(1)} %bitcast.8) | data formatting | bytes 589824
Async XLA Ops:
  1.3 1.7 %copy-start = (bf16[512,2304]{1,0:T(8,128)(2,1)S(1)}, bf16[512,2304]{1,0:T(8,128)(2,1)}, u32[]{:S(2)}) copy-start(bf16[512,2304]{1,0:T(8,128)(2,1)} %hidden.1) | copy-start | bytes 7077892
  3.0 1.0 %copy-start.1 = (bf16[512,288]{0,1:T(8,128)(2,1)S(1)}, bf16[512,288]{0,1:T(8,128)(2,1)}, u32[]{:S(2)}) copy-start(bf16[512,288]{0,1:T(8,128)(2,1)} %param.8) | copy-start | bytes 884740
  3.9 1.0 %copy-start.2 = (f32[2304,32]{0,1:T(8,128)S(1)}, f32[2304,32]{0,1:T(8,128)}, u32[]{:S(2)}) copy-start(f32[2304,32]{0,1:T(8,128)} %param.13) | copy-start | bytes 884740
  4.9 0.7 copy-start.3
  5.6 0.7 copy-start.4

commit v2 on v1

--- a/solution.py
+++ b/solution.py
@@ -15,7 +15,7 @@
 WIDTH = 288
 Z = 8
 NDP = 32
-OWNERS = 24
+GROUP = 4
 CH = 384
 PARTS = 9
 PART = D // PARTS
@@ -53,6 +53,14 @@
 
 def mm_t(a, b):
     return lax.dot_general(a, b, (((1,), (1,)), ((), ())), preferred_element_type=F32)
+
+
+def pack(x):
+    return jnp.concatenate([x[8 * i : 8 * i + 8] for i in range(4)], axis=1)
+
+
+def unpack(x):
+    return jnp.concatenate([x[:, 32 * i : 32 * i + 32] for i in range(4)], axis=0)
 
 
 def column(row):
@@ -78,12 +86,12 @@
 def kernel(
     hidden, upstream_t, head, margins, ends_t, error, q_t,
     basis_out, proj_out,
-    h, e, u, hd, mg, en, q, q2, cot, c128,
+    h, h_t, e, u, hd, mg, en, q, q2, cot, c128,
     p_part, p_in, p_red, p_full,
     f_part, f_in, f_red, f_full,
     w_part, w_in, g_part, g_in,
-    s_part, s_in, s_red, z_in, s_tot, s_full, b_out, r_out,
-    load, e_load, out_sem,
+    s_part, s_in, s_red, z_in, s_tot, s_full,
+    load, e_load,
     p_s, p_r, pg_s, pg_r, c_s, c_r, f_s, f_r, fg_s, fg_r,
     w_s, w_r, g_s, g_r, s_s, s_r, zs_s, zs_r, sg_s, sg_r,
 ):
@@ -130,15 +138,17 @@
         pltpu.make_async_copy(error.at[0, pl.ds(PART * i, PART)], e.at[pl.ds(PART * i, PART)], e_load.at[i])
         for i in range(PARTS)
     ]
-    for c in loads[:5] + e_loads + loads[5:]:
+    for c in loads[:5]:
         c.start()
 
     barrier = pltpu.get_barrier_semaphore()
+    for step in LINE:
+        pl.semaphore_signal(barrier, inc=1, device_id={"mp": along(step)}, device_id_type=MESH)
     for o in PLANE:
         y, x, c = away(o)
         pl.semaphore_signal(barrier, inc=1, device_id={"dp": (y * 4 + x) * 2 + c}, device_id_type=MESH)
-    for step in LINE:
-        pl.semaphore_signal(barrier, inc=1, device_id={"mp": along(step)}, device_id_type=MESH)
+    for c in e_loads + loads[5:]:
+        c.start()
 
     shift = pl.multiple_of(lax.rem(z, 4) * 32, 32)
     window = pl.multiple_of((2 * z + lax.div(z, 4)) * 128, 128)
@@ -153,7 +163,7 @@
         axis=0,
         keepdims=True,
     )
-    direction = jnp.broadcast_to(hd[...], (128, WIDTH)).T[:, :1]
+    direction = jnp.broadcast_to(hd[...].reshape(1, WIDTH), (128, WIDTH)).T[:, :1]
     cot[pl.ds(shift, WIDTH), :] = (u[...].astype(F32) + direction * weight).astype(BF16)
     q2[...] = split(q[...])
     p_part[...] = fold(mm(q2[:, pl.ds(window, CH)], cot[...]))
@@ -168,10 +178,12 @@
     ]
     for c in p_sends:
         c.start()
-    for i in range(PARTS):
-        e_loads[i].wait()
-        f_part[:, PART * i : PART * (i + 1)] = fold(mm_t(q2[...], e[PART * i : PART * (i + 1), :]))
-    loads[5].wait()
+    def error_part(first, last):
+        for i in range(first, last):
+            e_loads[i].wait()
+            f_part[:, PART * i : PART * (i + 1)] = fold(mm_t(q2[...], e[PART * i : PART * (i + 1), :]))
+
+    error_part(0, 5)
     arrived(p_in, p_r)
     total = p_chunk(p_part, z)[...]
     for j in range(Z - 1):
@@ -186,15 +198,14 @@
         return ref.at[pl.ds(pl.multiple_of(z * WIDTH, 32), WIDTH)]
 
     def c_lanes(t):
-        lane = pl.multiple_of(lax.div(t, 2) * 128, 128)
+        lane = pl.multiple_of(lax.rem(t, GROUP) * 128, 128)
         return cot.at[pl.ds(shift, WIDTH), pl.ds(lane, 128)]
 
     c_sends = [
         remote(c_lanes(along(o)), c_rows(c128), c_s.at[j], c_r, mp=along(o)) for j, o in enumerate(LINE)
     ]
-    for c in c_sends:
-        c.start()
-    pltpu.make_async_copy(c_lanes(z), c_rows(c128), c_r).start()
+    error_part(5, PARTS)
+    loads[5].wait()
     for c in p_sends:
         c.wait_send()
     arrived(p_full, pg_r)
@@ -231,8 +242,12 @@
                 copy.wait_send()
 
     to_owners(f_part, f_in, f_s, f_r, True)
-    for c in pg_sends + c_sends:
+    for c in c_sends:
+        c.start()
+    pltpu.make_async_copy(c_lanes(z), c_rows(c128), c_r).start()
+    for c in pg_sends:
         c.wait_send()
+    h_t[...] = h[...].T
 
     @pl.when(is_owner)
     def _():
@@ -241,60 +256,59 @@
         pltpu.make_async_copy(f_red, chunk(f_full, mine), fg_r).start()
 
     to_owners(f_part, f_in, f_s, f_r, False)
+    arrived(f_full, fg_r)
+
+    f2 = split(f_full[...])
+    w_part[...] = fold(mm(f2, h_t[...]))
+
+    def w_chunk(ref, t):
+        return ref.at[:, pl.ds(pl.multiple_of(lax.rem(t, GROUP) * 128, 128), 128)]
+
+    def near(step):
+        return lax.div(z, GROUP) * GROUP + lax.rem(z + step, GROUP)
+
+    w_sends = [
+        remote(w_chunk(w_part, near(j + 1)), w_in.at[j], w_s.at[j], w_r, mp=near(j + 1)) for j in range(GROUP - 1)
+    ]
+    for c in w_sends:
+        c.start()
+    s_part[...] = fold(mm(f2, e[...]))
     arrived(c128, c_r)
-    arrived(f_full, fg_r)
-
-    f2 = split(f_full[...])
-    w_part[...] = fold(mm_t(f2, h[...]))
-
-    def w_chunk(ref, t):
-        row = pl.multiple_of(lax.rem(t, 2) * 16, 16)
-        return ref.at[pl.ds(row, 16), pl.ds(pl.multiple_of(lax.div(t, 2) * 128, 128), 128)]
-
-    w_sends = [
-        remote(w_chunk(w_part, along(o)), w_in.at[j], w_s.at[j], w_r, mp=along(o)) for j, o in enumerate(LINE)
-    ]
-    for c in w_sends:
-        c.start()
+    arrived(w_in, w_r)
+    total = w_chunk(w_part, z)[...]
+    for j in range(GROUP - 1):
+        total += w_in[j]
+    s_part[...] += fold(mm_t(split(total), c128[...]))
+    to_owners(s_part, s_in, s_s, s_r, True)
     gram = mm_t(f2, f2)
-    g_part[...] = fold(gram[:, :RANK] + gram[:, RANK:])
+    g_part[...] = pack(fold(gram[:, :RANK] + gram[:, RANK:]))
     g_sends = [remote(g_part, g_in.at[z], g_s.at[j], g_r, mp=along(o)) for j, o in enumerate(LINE)]
     for c in g_sends:
         c.start()
     pltpu.make_async_copy(g_part, g_in.at[z], g_r).start()
 
-    s_part[...] = fold(mm(f2, e[...]))
+    for c in c_sends + w_sends + g_sends:
+        c.wait_send()
 
     @pl.when(is_owner)
     def _():
         hand_round(f_red, f_full, fg_s, fg_r, False)
 
-    for c in w_sends + g_sends:
-        c.wait_send()
-    arrived(w_in, w_r)
-    total = w_chunk(w_part, z)[...]
-    for j in range(Z - 1):
-        total += w_in[j]
-    half = pl.ds(pl.multiple_of(lax.rem(z, 2) * 16, 16), 16)
-    s_part[half, :] += fold(mm_t(split(total), c128[...]))
-
-    to_owners(s_part, s_in, s_s, s_r, True)
+    @pl.when(is_owner)
+    def _():
+        s_red[...] = add_up(s_part, s_in, s_r)
+
+        for j, o in enumerate(LINE):
+            remote(s_red, z_in.at[z], zs_s.at[j], zs_r, mp=along(o)).start()
+        pltpu.make_async_copy(s_red, z_in.at[z], zs_r).start()
+
     arrived(g_in, g_r)
     total = g_in[0]
     for j in range(1, Z):
         total += g_in[j]
-    inverse = inverse_lower(total)
-
-    @pl.when(is_owner)
-    def _():
-        s_red[...] = add_up(s_part, s_in, s_r)
-        for j, o in enumerate(LINE):
-            remote(s_red, z_in.at[z], zs_s.at[j], zs_r, mp=along(o)).start()
-        pltpu.make_async_copy(s_red, z_in.at[z], zs_r).start()
-
-    b_out[...] = jnp.dot(inverse * math.sqrt(FF), f_full[...], precision=HI, preferred_element_type=F32)
-    out = pltpu.make_async_copy(b_out, basis_out, out_sem.at[0])
-    out.start()
+    inverse = inverse_lower(unpack(total))
+
+    basis_out[...] = jnp.dot(inverse * math.sqrt(FF), f_full[...], precision=HI, preferred_element_type=F32)
 
     @pl.when(is_owner)
     def _():
@@ -310,41 +324,36 @@
 
     to_owners(s_part, s_in, s_s, s_r, False)
     arrived(s_full, sg_r)
-    r_out[...] = jnp.dot(inverse * (1.0 / NDP), s_full[...], precision=HI, preferred_element_type=F32)
-    last = pltpu.make_async_copy(r_out, proj_out, out_sem.at[1])
-    last.start()
+    proj_out[...] = jnp.dot(inverse * (1.0 / NDP), s_full[...], precision=HI, preferred_element_type=F32)
 
     @pl.when(is_owner)
     def _():
         hand_round(s_tot, s_full, sg_s, sg_r, False)
 
-    out.wait()
-    last.wait()
-
 
 def shards(hidden, upstream, reward_head, margins, ends, residual_error, previous_q):
-    any_spec = pl.BlockSpec(memory_space=pl.ANY)
+    hbm_spec = pl.BlockSpec(memory_space=pltpu.HBM)
+    vmem_spec = pl.BlockSpec(memory_space=pltpu.VMEM)
     vmem, dma = pltpu.VMEM, pltpu.SemaphoreType.DMA
-    whole = jax.ShapeDtypeStruct((RANK, D), F32)
-    line, plane, one = dma((Z - 1,)), dma((NDP - 1,)), dma(())
+    whole = vmem((RANK, D), F32)
+    line, plane, few, one = dma((Z - 1,)), dma((NDP - 1,)), dma((GROUP - 1,)), dma(())
     basis, projection = pl.pallas_call(
         kernel,
         out_shape=(whole, whole),
-        in_specs=[any_spec] * 7,
-        out_specs=(any_spec, any_spec),
+        in_specs=[hbm_spec] * 7,
+        out_specs=(vmem_spec, vmem_spec),
         scratch_shapes=[
-            vmem((TOK, D), BF16), vmem((D, D), BF16), vmem((WIDTH, TOK), BF16), vmem((1, WIDTH), F32),
+            vmem((TOK, D), BF16), vmem((D, TOK), BF16), vmem((D, D), BF16), vmem((WIDTH, TOK), BF16), vmem((WIDTH,), F32),
             vmem((1, PAIRS), F32), vmem((2, PAIRS), jnp.int32), vmem((RANK, D), F32), vmem((2 * RANK, D), BF16),
             vmem((CH, TOK), BF16), vmem((D, 128), BF16),
             vmem((RANK, TOK), F32), vmem((Z - 1, 8, 256), F32), vmem((8, 256), F32), vmem((RANK, TOK), F32),
             vmem((RANK, D), F32), vmem((NDP - 1, 8, CH), F32), vmem((8, CH), F32), vmem((RANK, D), F32),
-            vmem((RANK, TOK), F32), vmem((Z - 1, 16, 128), F32),
-            vmem((RANK, RANK), F32), vmem((Z, RANK, RANK), F32),
-            vmem((RANK, D), F32), vmem((NDP - 1, 8, CH), F32), vmem((8, CH), F32), vmem((Z, 8, CH), F32),
-            vmem((8, CH), F32), vmem((RANK, D), F32), vmem((RANK, D), F32), vmem((RANK, D), F32),
-            dma((6,)), dma((PARTS,)), dma((2,)),
+            vmem((RANK, TOK), F32), vmem((GROUP - 1, RANK, 128), F32),
+            vmem((8, 128), F32), vmem((Z, 8, 128), F32),
+            vmem((RANK, D), F32), vmem((NDP - 1, 8, CH), F32), vmem((8, CH), F32), vmem((Z, 8, CH), F32), vmem((8, CH), F32), vmem((RANK, D), F32),
+            dma((6,)), dma((PARTS,)),
             line, one, line, one, line, one, plane, one, plane, one,
-            line, one, line, one, plane, one, line, one, plane, one,
+            few, one, line, one, plane, one, line, one, plane, one,
         ],
         compiler_params=pltpu.CompilerParams(
             collective_id=0, has_side_effects=True, vmem_limit_bytes=48 * 1024 * 1024
@@ -352,8 +361,12 @@
         cost_estimate=pl.CostEstimate(flops=2_000_000_000, bytes_accessed=14_000_000, transcendentals=0),
         name="power_step",
     )(
-        hidden, upstream.T, reward_head.reshape(1, WIDTH), margins.reshape(1, PAIRS), ends.T, residual_error,
-        previous_q.T,
+        *(
+            pltpu.with_memory_space_constraint(x, pltpu.HBM)
+            for x in (
+                hidden, upstream.T, reward_head, margins.reshape(1, PAIRS), ends.T, residual_error, previous_q.T
+            )
+        )
     )
     return basis.T, projection.T
 

time: 70.9 us -> 58.9 us (0.83)
  Pallas kernels: 63 us -> 56.7 us
  local copies, waits for them, and re-layouts: 7.03 us -> 1.43 us
    pallas_call x1, Pallas kernels: 63 us -> 56.7 us  [shards(): pl.pallas_call(kernel, out_shape=(whole, whole), in_specs=[hbm_spec] * 7,...]
    unnamed x12 -> x2, local copies, waits for them, and re-layouts: 6.35 us -> 1.43 us
where the time goes in v2:
time: 58.9 us; the launch traced here: 58.8 us
  Pallas kernels  56.7 us (96%)
  local copies, waits for them, and re-layouts  1.43 us (2%)
  between operations  0.64 us (1%)
    pallas_call x1, Pallas kernels, shards(): pl.pallas_call(kernel, out_shape=(whole, whole), in_specs=[hbm_spec] * 7,...  56.7 us
    unnamed x2, local copies, waits for them, and re-layouts  1.43 us

profile of v2, /device:TPU:1, one launch (start us, length us, event | category | flops | bytes accessed | tf_op | source)
XLA Modules:
  0.0 58.8 jit_solution(4248099310437832982)
XLA Ops:
  0.6 56.7 %power_step.1 = (f32[32,2304]{1,0:T(8,128)S(1)}, f32[32,2304]{1,0:T(8,128)S(1)}) custom-call(bf16[512,2304]{1,0:T(8,128)(2,1)} %hidden.1, bf16[288,512]{1,0:T(8,128)(2,1)} %bitcast.8, f32[288]{0:T(512)} %head.1, f32[1,16]{1,0:T(1,128)} %bitcast.11, s32[2,16]{1,0:T(2,128)} %bitcast.10, bf16[1,2304,2304]{2,1,0:T(8,128)(2,1)} %error.1, f32[32,2304]{1,0:T(8,128)} %bitcast.9), custom_call_target="tpu_custom_call" | custom-call | flops 2000000000 | bytes 14000000 | tf_op jit(solution)/shard_map/power_step/pallas_call | solution.py:340
  57.4 0.7 %copy.11 = f32[2304,32]{0,1:T(8,128)} copy(f32[2304,32]{0,1:T(8,128)S(1)} %bitcast.7) | data formatting | bytes 589824
  58.1 0.7 %copy.12 = f32[2304,32]{0,1:T(8,128)} copy(f32[2304,32]{0,1:T(8,128)S(1)} %bitcast.6) | data formatting | bytes 589824

commit v3 on v2

--- a/solution.py
+++ b/solution.py
@@ -16,11 +16,11 @@
 Z = 8
 NDP = 32
 GROUP = 4
+OWNERS = 24
 CH = 384
 PARTS = 9
 PART = D // PARTS
 MESH = pl.DeviceIdType.MESH
-HI = lax.Precision.HIGHEST
 F32 = jnp.float32
 BF16 = jnp.bfloat16
 
@@ -61,6 +61,22 @@
 
 def unpack(x):
     return jnp.concatenate([x[:, 32 * i : 32 * i + 32] for i in range(4)], axis=0)
+
+
+def thirds(x):
+    high = x.astype(BF16).astype(F32)
+    middle = (x - high).astype(BF16).astype(F32)
+    return high, middle, (x - high - middle).astype(BF16).astype(F32)
+
+
+def left_terms(x):
+    high, middle, low = thirds(x)
+    return jnp.concatenate([high, high, middle, high, middle, low], axis=1).astype(BF16)
+
+
+def right_terms(x):
+    high, middle, low = (t.astype(BF16) for t in thirds(x))
+    return jnp.concatenate([high, middle, high, low, middle, high], axis=0)
 
 
 def column(row):
@@ -85,7 +101,7 @@
 
 def kernel(
     hidden, upstream_t, head, margins, ends_t, error, q_t,
-    basis_out, proj_out,
+    both,
     h, h_t, e, u, hd, mg, en, q, q2, cot, c128,
     p_part, p_in, p_red, p_full,
     f_part, f_in, f_red, f_full,
@@ -174,7 +190,7 @@
         return ref.at[pl.ds(row, 8), pl.ds(pl.multiple_of(lax.rem(t, 2) * 256, 128), 256)]
 
     p_sends = [
-        remote(p_chunk(p_part, along(o)), p_in.at[j], p_s.at[j], p_r, mp=along(o)) for j, o in enumerate(LINE)
+        remote(p_chunk(p_part, along(o)), p_in.at[j], p_s, p_r, mp=along(o)) for j, o in enumerate(LINE)
     ]
     for c in p_sends:
         c.start()
@@ -189,7 +205,7 @@
     for j in range(Z - 1):
         total += p_in[j]
     p_red[...] = total
-    pg_sends = [remote(p_red, p_chunk(p_full, z), pg_s.at[j], pg_r, mp=along(o)) for j, o in enumerate(LINE)]
+    pg_sends = [remote(p_red, p_chunk(p_full, z), pg_s, pg_r, mp=along(o)) for j, o in enumerate(LINE)]
     for c in pg_sends:
         c.start()
     pltpu.make_async_copy(p_red, p_chunk(p_full, z), pg_r).start()
@@ -202,28 +218,30 @@
         return cot.at[pl.ds(shift, WIDTH), pl.ds(lane, 128)]
 
     c_sends = [
-        remote(c_lanes(along(o)), c_rows(c128), c_s.at[j], c_r, mp=along(o)) for j, o in enumerate(LINE)
+        remote(c_lanes(along(o)), c_rows(c128), c_s, c_r, mp=along(o)) for j, o in enumerate(LINE)
     ]
     error_part(5, PARTS)
     loads[5].wait()
-    for c in p_sends:
-        c.wait_send()
+    arrived(p_in, p_s)
     arrived(p_full, pg_r)
     f_part[...] += fold(mm(split(p_full[...]), h[...]))
 
-    def to_owners(part, into, send, recv, start):
+    def to_owners(part, into, send, recv):
         for j, o in enumerate(PLANE):
             y, x, c = away(o)
 
             @pl.when(owns(y, x, c))
             def _(j=j, y=y, x=x, c=c):
-                copy = remote(
-                    chunk(part, owned(y, x, c)), into.at[j], send.at[j], recv, dp=(y * 4 + x) * 2 + c
-                )
-                if start:
-                    copy.start()
-                else:
-                    copy.wait_send()
+                remote(chunk(part, owned(y, x, c)), into.at[j], send, recv, dp=(y * 4 + x) * 2 + c).start()
+
+    def sent(into, send):
+        @pl.when(is_owner)
+        def _():
+            arrived(into.at[pl.ds(0, OWNERS - 1)], send)
+
+        @pl.when(jnp.logical_not(is_owner))
+        def _():
+            arrived(into.at[pl.ds(0, OWNERS)], send)
 
     def add_up(part, into, recv):
         arrived(into, recv)
@@ -232,30 +250,25 @@
             total += into[j]
         return total
 
-    def hand_round(red, full, send, recv, start):
-        for j, o in enumerate(PLANE):
+    def hand_round(red, full, send, recv):
+        for o in PLANE:
             y, x, c = away(o)
-            copy = remote(red, chunk(full, mine), send.at[j], recv, dp=(y * 4 + x) * 2 + c)
-            if start:
-                copy.start()
-            else:
-                copy.wait_send()
-
-    to_owners(f_part, f_in, f_s, f_r, True)
+            remote(red, chunk(full, mine), send, recv, dp=(y * 4 + x) * 2 + c).start()
+        pltpu.make_async_copy(red, chunk(full, mine), recv).start()
+
+    to_owners(f_part, f_in, f_s, f_r)
     for c in c_sends:
         c.start()
     pltpu.make_async_copy(c_lanes(z), c_rows(c128), c_r).start()
-    for c in pg_sends:
-        c.wait_send()
+    arrived(p_in, pg_s)
     h_t[...] = h[...].T
 
     @pl.when(is_owner)
     def _():
         f_red[...] = add_up(f_part, f_in, f_r)
-        hand_round(f_red, f_full, fg_s, fg_r, True)
-        pltpu.make_async_copy(f_red, chunk(f_full, mine), fg_r).start()
-
-    to_owners(f_part, f_in, f_s, f_r, False)
+        hand_round(f_red, f_full, fg_s, fg_r)
+
+    sent(f_in, f_s)
     arrived(f_full, fg_r)
 
     f2 = split(f_full[...])
@@ -268,7 +281,7 @@
         return lax.div(z, GROUP) * GROUP + lax.rem(z + step, GROUP)
 
     w_sends = [
-        remote(w_chunk(w_part, near(j + 1)), w_in.at[j], w_s.at[j], w_r, mp=near(j + 1)) for j in range(GROUP - 1)
+        remote(w_chunk(w_part, near(j + 1)), w_in.at[j], w_s, w_r, mp=near(j + 1)) for j in range(GROUP - 1)
     ]
     for c in w_sends:
         c.start()
@@ -279,27 +292,28 @@
     for j in range(GROUP - 1):
         total += w_in[j]
     s_part[...] += fold(mm_t(split(total), c128[...]))
-    to_owners(s_part, s_in, s_s, s_r, True)
+    to_owners(s_part, s_in, s_s, s_r)
     gram = mm_t(f2, f2)
     g_part[...] = pack(fold(gram[:, :RANK] + gram[:, RANK:]))
-    g_sends = [remote(g_part, g_in.at[z], g_s.at[j], g_r, mp=along(o)) for j, o in enumerate(LINE)]
+    g_sends = [remote(g_part, g_in.at[z], g_s, g_r, mp=along(o)) for j, o in enumerate(LINE)]
     for c in g_sends:
         c.start()
     pltpu.make_async_copy(g_part, g_in.at[z], g_r).start()
 
-    for c in c_sends + w_sends + g_sends:
-        c.wait_send()
-
-    @pl.when(is_owner)
-    def _():
-        hand_round(f_red, f_full, fg_s, fg_r, False)
+    arrived(c128.at[pl.ds(0, 7 * WIDTH)], c_s)
+    arrived(w_in, w_s)
+    arrived(g_in.at[pl.ds(0, Z - 1)], g_s)
+
+    @pl.when(is_owner)
+    def _():
+        arrived(f_in, fg_s)
 
     @pl.when(is_owner)
     def _():
         s_red[...] = add_up(s_part, s_in, s_r)
 
         for j, o in enumerate(LINE):
-            remote(s_red, z_in.at[z], zs_s.at[j], zs_r, mp=along(o)).start()
+            remote(s_red, z_in.at[z], zs_s, zs_r, mp=along(o)).start()
         pltpu.make_async_copy(s_red, z_in.at[z], zs_r).start()
 
     arrived(g_in, g_r)
@@ -308,7 +322,8 @@
         total += g_in[j]
     inverse = inverse_lower(unpack(total))
 
-    basis_out[...] = jnp.dot(inverse * math.sqrt(FF), f_full[...], precision=HI, preferred_element_type=F32)
+    left = left_terms(inverse)
+    both[:RANK] = mm(left, right_terms(f_full[...]))
 
     @pl.when(is_owner)
     def _():
@@ -317,31 +332,27 @@
         for j in range(1, Z):
             total += z_in[j]
         s_tot[...] = total
-        hand_round(s_tot, s_full, sg_s, sg_r, True)
-        pltpu.make_async_copy(s_tot, chunk(s_full, mine), sg_r).start()
-        for j, o in enumerate(LINE):
-            remote(s_red, z_in.at[z], zs_s.at[j], zs_r, mp=along(o)).wait_send()
-
-    to_owners(s_part, s_in, s_s, s_r, False)
+        hand_round(s_tot, s_full, sg_s, sg_r)
+        arrived(z_in.at[pl.ds(0, Z - 1)], zs_s)
+
+    sent(s_in, s_s)
     arrived(s_full, sg_r)
-    proj_out[...] = jnp.dot(inverse * (1.0 / NDP), s_full[...], precision=HI, preferred_element_type=F32)
-
-    @pl.when(is_owner)
-    def _():
-        hand_round(s_tot, s_full, sg_s, sg_r, False)
+    both[RANK:] = mm(left, right_terms(s_full[...]))
+
+    @pl.when(is_owner)
+    def _():
+        arrived(s_in, sg_s)
 
 
 def shards(hidden, upstream, reward_head, margins, ends, residual_error, previous_q):
     hbm_spec = pl.BlockSpec(memory_space=pltpu.HBM)
     vmem_spec = pl.BlockSpec(memory_space=pltpu.VMEM)
     vmem, dma = pltpu.VMEM, pltpu.SemaphoreType.DMA
-    whole = vmem((RANK, D), F32)
-    line, plane, few, one = dma((Z - 1,)), dma((NDP - 1,)), dma((GROUP - 1,)), dma(())
-    basis, projection = pl.pallas_call(
+    both = pl.pallas_call(
         kernel,
-        out_shape=(whole, whole),
+        out_shape=vmem((2 * RANK, D), F32),
         in_specs=[hbm_spec] * 7,
-        out_specs=(vmem_spec, vmem_spec),
+        out_specs=vmem_spec,
         scratch_shapes=[
             vmem((TOK, D), BF16), vmem((D, TOK), BF16), vmem((D, D), BF16), vmem((WIDTH, TOK), BF16), vmem((WIDTH,), F32),
             vmem((1, PAIRS), F32), vmem((2, PAIRS), jnp.int32), vmem((RANK, D), F32), vmem((2 * RANK, D), BF16),
@@ -352,8 +363,7 @@
             vmem((8, 128), F32), vmem((Z, 8, 128), F32),
             vmem((RANK, D), F32), vmem((NDP - 1, 8, CH), F32), vmem((8, CH), F32), vmem((Z, 8, CH), F32), vmem((8, CH), F32), vmem((RANK, D), F32),
             dma((6,)), dma((PARTS,)),
-            line, one, line, one, line, one, plane, one, plane, one,
-            few, one, line, one, plane, one, line, one, plane, one,
+            *[dma(())] * 20,
         ],
         compiler_params=pltpu.CompilerParams(
             collective_id=0, has_side_effects=True, vmem_limit_bytes=48 * 1024 * 1024
@@ -368,7 +378,7 @@
             )
         )
     )
-    return basis.T, projection.T
+    return both[:RANK].T * math.sqrt(FF), both[RANK:].T * (1.0 / NDP)
 
 
 def solution(mesh):

time: 58.9 us -> 56.6 us (0.961)
  Pallas kernels: 56.7 us -> 55 us
  local copies, waits for them, and re-layouts: 1.43 us -> 0 us
  other arithmetic: 0 us -> 0.86 us
    pallas_call x1, Pallas kernels: 56.7 us -> 55 us  [shards(): pl.pallas_call(kernel, out_shape=vmem((2 * RANK, D), F32), in_specs=[hbm_...]
    unnamed x2 -> x0, local copies, waits for them, and re-layouts: 1.43 us -> none
    mul x0 -> x1, other arithmetic: none -> 0.86 us  [shards(): return (both[:RANK].T * math.sqrt(FF), both[RANK:].T * (1.0 / NDP))]
where the time goes in v3:
time: 56.6 us; the launch traced here: 56.5 us
  Pallas kernels  55 us (97%)
  other arithmetic  0.86 us (2%)
  between operations  0.64 us (1%)
    pallas_call x1, Pallas kernels, shards(): pl.pallas_call(kernel, out_shape=vmem((2 * RANK, D), F32), in_specs=[hbm_...  55 us

profile of v3, /device:TPU:1, one launch (start us, length us, event | category | flops | bytes accessed | tf_op | source)
XLA Modules:
  0.0 56.5 jit_solution(4176878887350742315)
XLA Ops:
  0.6 55.0 %power_step.1 = f32[64,2304]{1,0:T(8,128)S(1)} custom-call(bf16[512,2304]{1,0:T(8,128)(2,1)} %hidden.1, bf16[288,512]{1,0:T(8,128)(2,1)} %bitcast.8, f32[288]{0:T(512)} %head.1, f32[1,16]{1,0:T(1,128)} %bitcast.11, s32[2,16]{1,0:T(2,128)} %bitcast.10, bf16[1,2304,2304]{2,1,0:T(8,128)(2,1)} %error.1, f32[32,2304]{1,0:T(8,128)} %bitcast.9), custom_call_target="tpu_custom_call" | custom-call | flops 2000000000 | bytes 14000000 | tf_op jit(solution)/shard_map/power_step/pallas_call | solution.py:351
  55.7 0.9 %multiply_bitcast_fusion = (f32[2304,32]{0,1:T(8,128)}, f32[2304,32]{0,1:T(8,128)}) fusion(f32[64,2304]{1,0:T(8,128)S(1)} %power_step.1), kind=kLoop, calls=%fused_computation | loop fusion | flops 147456 | bytes 1179648 | tf_op jit(solution)/shard_map/mul | solution.py:381

commit v4 on v3

--- a/solution.py
+++ b/solution.py
@@ -15,7 +15,7 @@
 WIDTH = 288
 Z = 8
 NDP = 32
-GROUP = 4
+HALF = WIDTH // 2
 OWNERS = 24
 CH = 384
 PARTS = 9
@@ -33,6 +33,7 @@
     ((dy, dx, dc) for dy in range(4) for dx in range(4) for dc in range(2) if (dy, dx, dc) != (0, 0, 0)),
     key=lambda o: -(ring(o[0], 4) + ring(o[1], 4)),
 )
+CHIPS = [o[:2] for o in PLANE if o[2] == 0]
 LINE = (4, 3, 5, 2, 6, 1, 7)
 
 
@@ -77,6 +78,11 @@
 def right_terms(x):
     high, middle, low = (t.astype(BF16) for t in thirds(x))
     return jnp.concatenate([high, middle, high, low, middle, high], axis=0)
+
+
+def interleave(a, b):
+    low = lax.broadcasted_iota(jnp.int32, a.shape, 1) < 64
+    return jnp.where(low, a, pltpu.roll(b, 64, 1)), jnp.where(low, pltpu.roll(a, 64, 1), b)
 
 
 def column(row):
@@ -102,28 +108,26 @@
 def kernel(
     hidden, upstream_t, head, margins, ends_t, error, q_t,
     both,
-    h, h_t, e, u, hd, mg, en, q, q2, cot, c128,
+    h, h_t, e, u, hd, mg, en, q, q2, cot, cot_x, c_pack, c_all,
     p_part, p_in, p_red, p_full,
-    f_part, f_in, f_red, f_full,
-    w_part, w_in, g_part, g_in,
-    s_part, s_in, s_red, z_in, s_tot, s_full,
+    f_part, f_other, f_in, f_red, f_full,
+    w_part, w_pack, w_in, g_part, g_in,
+    s_part, s_other, s_in, s_red, z_in, s_tot, s_full,
     load, e_load,
     p_s, p_r, pg_s, pg_r, c_s, c_r, f_s, f_r, fg_s, fg_r,
     w_s, w_r, g_s, g_r, s_s, s_r, zs_s, zs_r, sg_s, sg_r,
+    hx_s, hx_r, fx_s, fx_r, cx_s, cx_r, cf_s, cf_r, sx_s, sx_r,
 ):
     dp, z = lax.axis_index("dp"), lax.axis_index("mp")
     core, chip = lax.rem(dp, 2), lax.div(dp, 2)
     cy, cx = lax.div(chip, 4), lax.rem(chip, 4)
 
-    def owns(y, x, c):
-        return jnp.logical_or(c == 0, lax.rem(x + y, 2) == 0)
-
-    def owned(y, x, c):
-        place = y * 4 + x
-        return jnp.where(c == 0, place, 16 + lax.div(place, 2))
-
-    def chunk(ref, k):
-        row = pl.multiple_of(lax.div(k, 6) * 8, 8)
+    def place(y, x):
+        return lax.rem(x + y + 2 * core, 4)
+
+    def chunk(ref, y, x):
+        k = 3 * y + place(y, x) - 1
+        row = pl.multiple_of(16 * core + lax.div(k, 6) * 8, 8)
         lane = pl.multiple_of(lax.rem(k, 6) * CH, 128)
         return ref.at[pl.ds(row, 8), pl.ds(lane, CH)]
 
@@ -134,7 +138,10 @@
     def along(step):
         return lax.rem(z + step, Z)
 
-    is_owner, mine = owns(cy, cx, core), owned(cy, cx, core)
+    is_owner = place(cy, cx) != 0
+    own_half = pl.ds(pl.multiple_of(16 * core, 16), 16)
+    other_half = pl.ds(pl.multiple_of(16 * (1 - core), 16), 16)
+    sibling = dp + 1 - 2 * core
 
     def remote(src, dst, send, recv, **to):
         return pltpu.make_async_remote_copy(
@@ -147,7 +154,7 @@
     loads = [
         pltpu.make_async_copy(src, dst, load.at[i])
         for i, (src, dst) in enumerate(
-            [(upstream_t, u), (margins, mg), (ends_t, en), (head, hd), (q_t, q), (hidden, h)]
+            [(upstream_t, u), (margins, mg), (ends_t, en), (head, hd), (q_t, q), (hidden, h.at[pl.ds(0, TOK)])]
         )
     ]
     e_loads = [
@@ -160,6 +167,7 @@
     barrier = pltpu.get_barrier_semaphore()
     for step in LINE:
         pl.semaphore_signal(barrier, inc=1, device_id={"mp": along(step)}, device_id_type=MESH)
+        pl.semaphore_signal(barrier, inc=1, device_id={"dp": sibling, "mp": along(step)}, device_id_type=MESH)
     for o in PLANE:
         y, x, c = away(o)
         pl.semaphore_signal(barrier, inc=1, device_id={"dp": (y * 4 + x) * 2 + c}, device_id_type=MESH)
@@ -183,7 +191,10 @@
     cot[pl.ds(shift, WIDTH), :] = (u[...].astype(F32) + direction * weight).astype(BF16)
     q2[...] = split(q[...])
     p_part[...] = fold(mm(q2[:, pl.ds(window, CH)], cot[...]))
-    pl.semaphore_wait(barrier, NDP - 1 + Z - 1)
+    pl.semaphore_wait(barrier, NDP - 1 + 2 * (Z - 1))
+
+    def replicas(mine, other):
+        return jnp.where(core == 0, mine, other), jnp.where(core == 0, other, mine)
 
     def p_chunk(ref, t):
         row = pl.multiple_of(lax.div(t, 2) * 8, 8)
@@ -194,6 +205,11 @@
     ]
     for c in p_sends:
         c.start()
+    def c_half(c):
+        return cot.at[pl.ds(pl.multiple_of(shift + HALF * c, 16), HALF), :]
+
+    remote(c_half(1 - core), cot_x, cx_s, cx_r, dp=sibling).start()
+    remote(hidden, h.at[pl.ds(TOK, TOK)], hx_s, hx_r, dp=sibling).start()
     def error_part(first, last):
         for i in range(first, last):
             e_loads[i].wait()
@@ -205,63 +221,89 @@
     for j in range(Z - 1):
         total += p_in[j]
     p_red[...] = total
-    pg_sends = [remote(p_red, p_chunk(p_full, z), pg_s, pg_r, mp=along(o)) for j, o in enumerate(LINE)]
-    for c in pg_sends:
-        c.start()
-    pltpu.make_async_copy(p_red, p_chunk(p_full, z), pg_r).start()
-
-    def c_rows(ref):
-        return ref.at[pl.ds(pl.multiple_of(z * WIDTH, 32), WIDTH)]
-
-    def c_lanes(t):
-        lane = pl.multiple_of(lax.rem(t, GROUP) * 128, 128)
-        return cot.at[pl.ds(shift, WIDTH), pl.ds(lane, 128)]
-
-    c_sends = [
-        remote(c_lanes(along(o)), c_rows(c128), c_s, c_r, mp=along(o)) for j, o in enumerate(LINE)
-    ]
+    def p_place(slot):
+        row = pl.multiple_of(lax.rem(lax.div(z, 2), 2) * 8, 8)
+        return p_full.at[slot, pl.ds(row, 8), pl.ds(pl.multiple_of(lax.rem(z, 2) * 256, 128), 256)]
+
+    stays = lax.div(z, 4) == core
+
+    @pl.when(stays)
+    def _():
+        for o in LINE:
+            remote(p_red, p_place(0), pg_s, pg_r, mp=along(o)).start()
+        pltpu.make_async_copy(p_red, p_place(0), pg_r).start()
+
+    @pl.when(jnp.logical_not(stays))
+    def _():
+        for o in LINE:
+            remote(p_red, p_place(1), pg_s, pg_r, dp=sibling, mp=along(o)).start()
+        remote(p_red, p_place(1), pg_s, pg_r, dp=sibling).start()
+
+    def c_rows(t, c):
+        return c_all.at[pl.ds(pl.multiple_of(t * WIDTH + c * HALF, 16), HALF)]
+
     error_part(5, PARTS)
+    remote(f_part.at[other_half, :], f_other, fx_s, fx_r, dp=sibling).start()
+    arrived(cot_x, cx_r)
+    first, second = replicas(c_half(core)[...].astype(F32), cot_x[...].astype(F32))
+    for t in range(4):
+        even, odd = interleave(first[:, 128 * t : 128 * t + 128], second[:, 128 * t : 128 * t + 128])
+        c_pack[2 * t] = even.astype(BF16)
+        c_pack[2 * t + 1] = odd.astype(BF16)
     loads[5].wait()
     arrived(p_in, p_s)
+    arrived(h.at[pl.ds(TOK, TOK)], hx_r)
+    arrived(f_other, fx_r)
     arrived(p_full, pg_r)
-    f_part[...] += fold(mm(split(p_full[...]), h[...]))
+    probe = jnp.concatenate([p_full[0], p_full[1]], axis=1)
+    f_part[own_half, :] += f_other[...] + fold(mm(split(probe), h[...]))
 
     def to_owners(part, into, send, recv):
-        for j, o in enumerate(PLANE):
-            y, x, c = away(o)
-
-            @pl.when(owns(y, x, c))
-            def _(j=j, y=y, x=x, c=c):
-                remote(chunk(part, owned(y, x, c)), into.at[j], send, recv, dp=(y * 4 + x) * 2 + c).start()
+        for j, (dy, dx) in enumerate(CHIPS):
+            y, x = lax.rem(cy + dy, 4), lax.rem(cx + dx, 4)
+
+            @pl.when(place(y, x) != 0)
+            def _(j=j, y=y, x=x):
+                remote(chunk(part, y, x), into.at[j], send, recv, dp=y * 8 + x * 2 + core).start()
 
     def sent(into, send):
         @pl.when(is_owner)
         def _():
-            arrived(into.at[pl.ds(0, OWNERS - 1)], send)
+            arrived(into.at[pl.ds(0, OWNERS // 2 - 1)], send)
 
         @pl.when(jnp.logical_not(is_owner))
         def _():
-            arrived(into.at[pl.ds(0, OWNERS)], send)
+            arrived(into.at[pl.ds(0, OWNERS // 2)], send)
 
     def add_up(part, into, recv):
         arrived(into, recv)
-        total = chunk(part, mine)[...]
-        for j in range(NDP - 1):
+        total = chunk(part, cy, cx)[...]
+        for j in range(len(CHIPS)):
             total += into[j]
         return total
 
     def hand_round(red, full, send, recv):
         for o in PLANE:
             y, x, c = away(o)
-            remote(red, chunk(full, mine), send, recv, dp=(y * 4 + x) * 2 + c).start()
-        pltpu.make_async_copy(red, chunk(full, mine), recv).start()
+            remote(red, chunk(full, cy, cx), send, recv, dp=(y * 4 + x) * 2 + c).start()
+        pltpu.make_async_copy(red, chunk(full, cy, cx), recv).start()
 
     to_owners(f_part, f_in, f_s, f_r)
-    for c in c_sends:
-        c.start()
-    pltpu.make_async_copy(c_lanes(z), c_rows(c128), c_r).start()
-    arrived(p_in, pg_s)
-    h_t[...] = h[...].T
+    for o in LINE:
+        remote(c_pack.at[along(o)], c_rows(z, core), c_s, c_r, mp=along(o)).start()
+    pltpu.make_async_copy(c_pack.at[z], c_rows(z, core), c_r).start()
+    @pl.when(stays)
+    def _():
+        arrived(p_in, pg_s)
+
+    @pl.when(jnp.logical_not(stays))
+    def _():
+        arrived(p_in, pg_s)
+        arrived(p_in.at[0], pg_s)
+
+    arrived(f_other, fx_s)
+    arrived(h.at[pl.ds(0, TOK)], hx_s)
+    h_t[...] = h[pl.ds(0, TOK), :].T
 
     @pl.when(is_owner)
     def _():
@@ -269,29 +311,37 @@
         hand_round(f_red, f_full, fg_s, fg_r)
 
     sent(f_in, f_s)
+    arrived(c_all.at[pl.ds(0, Z * HALF)], c_r)
+    for t in range(Z):
+        remote(c_rows(t, core), c_rows(t, core), cf_s, cf_r, dp=sibling).start()
     arrived(f_full, fg_r)
 
     f2 = split(f_full[...])
     w_part[...] = fold(mm(f2, h_t[...]))
 
-    def w_chunk(ref, t):
-        return ref.at[:, pl.ds(pl.multiple_of(lax.rem(t, GROUP) * 128, 128), 128)]
-
-    def near(step):
-        return lax.div(z, GROUP) * GROUP + lax.rem(z + step, GROUP)
-
-    w_sends = [
-        remote(w_chunk(w_part, near(j + 1)), w_in.at[j], w_s, w_r, mp=near(j + 1)) for j in range(GROUP - 1)
-    ]
-    for c in w_sends:
-        c.start()
+    for half in range(2):
+        for t in range(4):
+            x = w_part[16 * half : 16 * half + 16, 128 * t : 128 * t + 128]
+            w_pack[half, 2 * t], w_pack[half, 2 * t + 1] = interleave(x[:8], x[8:])
+    for j, o in enumerate(LINE):
+        remote(w_pack.at[core, along(o)], w_in.at[j], w_s, w_r, mp=along(o)).start()
+        remote(w_pack.at[1 - core, along(o)], w_in.at[Z - 1 + j], w_s, w_r, dp=sibling, mp=along(o)).start()
+    remote(w_pack.at[1 - core, z], w_in.at[2 * Z - 2], w_s, w_r, dp=sibling).start()
     s_part[...] = fold(mm(f2, e[...]))
-    arrived(c128, c_r)
+    remote(s_part.at[other_half, :], s_other, sx_s, sx_r, dp=sibling).start()
+    arrived(c_all.at[pl.ds(0, Z * HALF)], cf_r)
     arrived(w_in, w_r)
-    total = w_chunk(w_part, z)[...]
-    for j in range(GROUP - 1):
+    total = w_pack[core, z]
+    for j in range(Z - 1):
         total += w_in[j]
-    s_part[...] += fold(mm_t(split(total), c128[...]))
+    other = w_in[Z - 1]
+    for j in range(Z, 2 * Z - 1):
+        other += w_in[j]
+    first, second = replicas(total, other)
+    tokens = jnp.concatenate(interleave(first, second), axis=0)
+    v = fold(mm_t(split(tokens), c_all[...]))
+    arrived(s_other, sx_r)
+    s_part[own_half, :] += s_other[...] + v
     to_owners(s_part, s_in, s_s, s_r)
     gram = mm_t(f2, f2)
     g_part[...] = pack(fold(gram[:, :RANK] + gram[:, RANK:]))
@@ -300,13 +350,18 @@
         c.start()
     pltpu.make_async_copy(g_part, g_in.at[z], g_r).start()
 
-    arrived(c128.at[pl.ds(0, 7 * WIDTH)], c_s)
+    arrived(c_pack.at[pl.ds(0, Z - 1)], c_s)
+    arrived(cot_x, cx_s)
+    arrived(c_all.at[pl.ds(0, Z * HALF)], cf_s)
+    arrived(s_other, sx_s)
     arrived(w_in, w_s)
     arrived(g_in.at[pl.ds(0, Z - 1)], g_s)
 
     @pl.when(is_owner)
     def _():
         arrived(f_in, fg_s)
+        arrived(f_in, fg_s)
+        arrived(f_in.at[0], fg_s)
 
     @pl.when(is_owner)
     def _():
@@ -342,6 +397,8 @@
     @pl.when(is_owner)
     def _():
         arrived(s_in, sg_s)
+        arrived(s_in, sg_s)
+        arrived(s_in.at[0], sg_s)
 
 
 def shards(hidden, upstream, reward_head, margins, ends, residual_error, previous_q):
@@ -354,16 +411,17 @@
         in_specs=[hbm_spec] * 7,
         out_specs=vmem_spec,
         scratch_shapes=[
-            vmem((TOK, D), BF16), vmem((D, TOK), BF16), vmem((D, D), BF16), vmem((WIDTH, TOK), BF16), vmem((WIDTH,), F32),
+            vmem((2 * TOK, D), BF16), vmem((D, TOK), BF16), vmem((D, D), BF16), vmem((WIDTH, TOK), BF16), vmem((WIDTH,), F32),
             vmem((1, PAIRS), F32), vmem((2, PAIRS), jnp.int32), vmem((RANK, D), F32), vmem((2 * RANK, D), BF16),
-            vmem((CH, TOK), BF16), vmem((D, 128), BF16),
-            vmem((RANK, TOK), F32), vmem((Z - 1, 8, 256), F32), vmem((8, 256), F32), vmem((RANK, TOK), F32),
-            vmem((RANK, D), F32), vmem((NDP - 1, 8, CH), F32), vmem((8, CH), F32), vmem((RANK, D), F32),
-            vmem((RANK, TOK), F32), vmem((GROUP - 1, RANK, 128), F32),
+            vmem((CH, TOK), BF16), vmem((HALF, TOK), BF16), vmem((Z, HALF, 128), BF16), vmem((D, 128), BF16),
+            vmem((RANK, TOK), F32), vmem((Z - 1, 8, 256), F32), vmem((8, 256), F32), vmem((2, 16, TOK), F32),
+            vmem((RANK, D), F32), vmem((16, D), F32), vmem((len(CHIPS), 8, CH), F32), vmem((8, CH), F32),
+            vmem((RANK, D), F32),
+            vmem((RANK, TOK), F32), vmem((2, Z, 8, 128), F32), vmem((2 * Z - 1, 8, 128), F32),
             vmem((8, 128), F32), vmem((Z, 8, 128), F32),
-            vmem((RANK, D), F32), vmem((NDP - 1, 8, CH), F32), vmem((8, CH), F32), vmem((Z, 8, CH), F32), vmem((8, CH), F32), vmem((RANK, D), F32),
+            vmem((RANK, D), F32), vmem((16, D), F32), vmem((len(CHIPS), 8, CH), F32), vmem((8, CH), F32), vmem((Z, 8, CH), F32), vmem((8, CH), F32), vmem((RANK, D), F32),
             dma((6,)), dma((PARTS,)),
-            *[dma(())] * 20,
+            *[dma(())] * 30,
         ],
         compiler_params=pltpu.CompilerParams(
             collective_id=0, has_side_effects=True, vmem_limit_bytes=48 * 1024 * 1024

time: 56.6 us -> 55.9 us (0.988)
  Pallas kernels: 55 us -> 54.4 us
    pallas_call x1, Pallas kernels: 55 us -> 54.4 us  [shards(): pl.pallas_call(kernel, out_shape=vmem((2 * RANK, D), F32), in_specs=[hbm_...]
where the time goes in v4:
time: 55.9 us
  Pallas kernels  54.4 us (97%)
  other arithmetic  0.86 us (2%)
  between operations  0.64 us (1%)
    pallas_call x1, Pallas kernels, shards(): pl.pallas_call(kernel, out_shape=vmem((2 * RANK, D), F32), in_specs=[hbm_...  54.4 us

profile of v4, /device:TPU:1, one launch (start us, length us, event | category | flops | bytes accessed | tf_op | source)
XLA Modules:
  0.0 55.9 jit_solution(13596006254135868254)
XLA Ops:
  0.6 54.4 %power_step.1 = f32[64,2304]{1,0:T(8,128)S(1)} custom-call(bf16[512,2304]{1,0:T(8,128)(2,1)} %hidden.1, bf16[288,512]{1,0:T(8,128)(2,1)} %bitcast.8, f32[288]{0:T(512)} %head.1, f32[1,16]{1,0:T(1,128)} %bitcast.11, s32[2,16]{1,0:T(2,128)} %bitcast.10, bf16[1,2304,2304]{2,1,0:T(8,128)(2,1)} %error.1, f32[32,2304]{1,0:T(8,128)} %bitcast.9), custom_call_target="tpu_custom_call" | custom-call | flops 2000000000 | bytes 14000000 | tf_op jit(solution)/shard_map/power_step/pallas_call | solution.py:408
  55.0 0.9 %multiply_bitcast_fusion = (f32[2304,32]{0,1:T(8,128)}, f32[2304,32]{0,1:T(8,128)}) fusion(f32[64,2304]{1,0:T(8,128)S(1)} %power_step.1), kind=kLoop, calls=%fused_computation | loop fusion | flops 147456 | bytes 1179648 | tf_op jit(solution)/shard_map/mul | solution.py:439

commit v5 on v4

--- a/solution.py
+++ b/solution.py
@@ -37,37 +37,35 @@
 LINE = (4, 3, 5, 2, 6, 1, 7)
 
 
-def split(x):
-    high = x.astype(BF16)
-    low = (x - high.astype(F32)).astype(BF16)
-    return jnp.concatenate([high, low], axis=0)
-
-
-def fold(x):
-    half = x.shape[0] // 2
-    return x[:half] + x[half:]
-
-
-def mm(a, b):
-    return lax.dot_general(a, b, (((1,), (0,)), ((), ())), preferred_element_type=F32)
-
-
-def mm_t(a, b):
-    return lax.dot_general(a, b, (((1,), (1,)), ((), ())), preferred_element_type=F32)
-
-
-def pack(x):
-    return jnp.concatenate([x[8 * i : 8 * i + 8] for i in range(4)], axis=1)
-
-
-def unpack(x):
-    return jnp.concatenate([x[:, 32 * i : 32 * i + 32] for i in range(4)], axis=0)
-
-
 def thirds(x):
     high = x.astype(BF16).astype(F32)
     middle = (x - high).astype(BF16).astype(F32)
     return high, middle, (x - high - middle).astype(BF16).astype(F32)
+
+
+def split(x):
+    return jnp.concatenate([t.astype(BF16) for t in thirds(x)], axis=0)
+
+
+def fold(x):
+    rows = x.shape[0] // 3
+    return x[:rows] + x[rows : 2 * rows] + x[2 * rows :]
+
+
+def mm(a, b):
+    return lax.dot_general(a, b, (((1,), (0,)), ((), ())), preferred_element_type=F32)
+
+
+def mm_t(a, b):
+    return lax.dot_general(a, b, (((1,), (1,)), ((), ())), preferred_element_type=F32)
+
+
+def pack(x):
+    return jnp.concatenate([x[8 * i : 8 * i + 8] for i in range(4)], axis=1)
+
+
+def unpack(x):
+    return jnp.concatenate([x[:, 32 * i : 32 * i + 32] for i in range(4)], axis=0)
 
 
 def left_terms(x):
@@ -344,7 +342,7 @@
     s_part[own_half, :] += s_other[...] + v
     to_owners(s_part, s_in, s_s, s_r)
     gram = mm_t(f2, f2)
-    g_part[...] = pack(fold(gram[:, :RANK] + gram[:, RANK:]))
+    g_part[...] = pack(fold(gram[:, :RANK] + gram[:, RANK : 2 * RANK] + gram[:, 2 * RANK :]))
     g_sends = [remote(g_part, g_in.at[z], g_s, g_r, mp=along(o)) for j, o in enumerate(LINE)]
     for c in g_sends:
         c.start()
@@ -412,7 +410,7 @@
         out_specs=vmem_spec,
         scratch_shapes=[
             vmem((2 * TOK, D), BF16), vmem((D, TOK), BF16), vmem((D, D), BF16), vmem((WIDTH, TOK), BF16), vmem((WIDTH,), F32),
-            vmem((1, PAIRS), F32), vmem((2, PAIRS), jnp.int32), vmem((RANK, D), F32), vmem((2 * RANK, D), BF16),
+            vmem((1, PAIRS), F32), vmem((2, PAIRS), jnp.int32), vmem((RANK, D), F32), vmem((3 * RANK, D), BF16),
             vmem((CH, TOK), BF16), vmem((HALF, TOK), BF16), vmem((Z, HALF, 128), BF16), vmem((D, 128), BF16),
             vmem((RANK, TOK), F32), vmem((Z - 1, 8, 256), F32), vmem((8, 256), F32), vmem((2, 16, TOK), F32),
             vmem((RANK, D), F32), vmem((16, D), F32), vmem((len(CHIPS), 8, CH), F32), vmem((8, CH), F32),

time: 55.9 us -> 55.6 us (level)
  no operation moved by 1% of the time
where the time goes in v5:
time: 55.6 us; the launch traced here: 55.5 us
  Pallas kernels  54 us (97%)
  other arithmetic  0.86 us (2%)
  between operations  0.64 us (1%)
    pallas_call x1, Pallas kernels, shards(): pl.pallas_call(kernel, out_shape=vmem((2 * RANK, D), F32), in_specs=[hbm_...  54 us

profile of v5, /device:TPU:1, one launch (start us, length us, event | category | flops | bytes accessed | tf_op | source)
XLA Modules:
  0.0 55.5 jit_solution(8105064066305661844)
XLA Ops:
  0.6 54.0 %power_step.1 = f32[64,2304]{1,0:T(8,128)S(1)} custom-call(bf16[512,2304]{1,0:T(8,128)(2,1)} %hidden.1, bf16[288,512]{1,0:T(8,128)(2,1)} %bitcast.8, f32[288]{0:T(512)} %head.1, f32[1,16]{1,0:T(1,128)} %bitcast.11, s32[2,16]{1,0:T(2,128)} %bitcast.10, bf16[1,2304,2304]{2,1,0:T(8,128)(2,1)} %error.1, f32[32,2304]{1,0:T(8,128)} %bitcast.9), custom_call_target="tpu_custom_call" | custom-call | flops 2000000000 | bytes 14000000 | tf_op jit(solution)/shard_map/power_step/pallas_call | solution.py:406
  54.6 0.9 %multiply_bitcast_fusion = (f32[2304,32]{0,1:T(8,128)}, f32[2304,32]{0,1:T(8,128)}) fusion(f32[64,2304]{1,0:T(8,128)S(1)} %power_step.1), kind=kLoop, calls=%fused_computation | loop fusion | flops 147456 | bytes 1179648 | tf_op jit(solution)/shard_map/mul | solution.py:437

commit v6 on v5

--- a/solution.py
+++ b/solution.py
@@ -159,9 +159,6 @@
         pltpu.make_async_copy(error.at[0, pl.ds(PART * i, PART)], e.at[pl.ds(PART * i, PART)], e_load.at[i])
         for i in range(PARTS)
     ]
-    for c in loads[:5]:
-        c.start()
-
     barrier = pltpu.get_barrier_semaphore()
     for step in LINE:
         pl.semaphore_signal(barrier, inc=1, device_id={"mp": along(step)}, device_id_type=MESH)
@@ -169,7 +166,7 @@
     for o in PLANE:
         y, x, c = away(o)
         pl.semaphore_signal(barrier, inc=1, device_id={"dp": (y * 4 + x) * 2 + c}, device_id_type=MESH)
-    for c in e_loads + loads[5:]:
+    for c in loads[:5] + e_loads + loads[5:]:
         c.start()
 
     shift = pl.multiple_of(lax.rem(z, 4) * 32, 32)
@@ -214,6 +211,8 @@
             f_part[:, PART * i : PART * (i + 1)] = fold(mm_t(q2[...], e[PART * i : PART * (i + 1), :]))
 
     error_part(0, 5)
+    early, late = pl.ds(0, 5 * PART), pl.ds(5 * PART, 4 * PART)
+    remote(f_part.at[other_half, early], f_other.at[:, early], fx_s, fx_r, dp=sibling).start()
     arrived(p_in, p_r)
     total = p_chunk(p_part, z)[...]
     for j in range(Z - 1):
@@ -241,7 +240,7 @@
         return c_all.at[pl.ds(pl.multiple_of(t * WIDTH + c * HALF, 16), HALF)]
 
     error_part(5, PARTS)
-    remote(f_part.at[other_half, :], f_other, fx_s, fx_r, dp=sibling).start()
+    remote(f_part.at[other_half, late], f_other.at[:, late], fx_s, fx_r, dp=sibling).start()
     arrived(cot_x, cx_r)
     first, second = replicas(c_half(core)[...].astype(F32), cot_x[...].astype(F32))
     for t in range(4):
@@ -251,10 +250,11 @@
     loads[5].wait()
     arrived(p_in, p_s)
     arrived(h.at[pl.ds(TOK, TOK)], hx_r)
-    arrived(f_other, fx_r)
     arrived(p_full, pg_r)
     probe = jnp.concatenate([p_full[0], p_full[1]], axis=1)
-    f_part[own_half, :] += f_other[...] + fold(mm(split(probe), h[...]))
+    leading = fold(mm(split(probe), h[...]))
+    arrived(f_other, fx_r)
+    f_part[own_half, :] += f_other[...] + leading
 
     def to_owners(part, into, send, recv):
         for j, (dy, dx) in enumerate(CHIPS):

time: 55.6 us -> 56.4 us (1.014)
  Pallas kernels: 54 us -> 54.8 us
    pallas_call x1, Pallas kernels: 54 us -> 54.8 us  [shards(): pl.pallas_call(kernel, out_shape=vmem((2 * RANK, D), F32), in_specs=[hbm_...]
where the time goes in v6:
time: 56.4 us; the launch traced here: 56.3 us
  Pallas kernels  54.8 us (97%)
  other arithmetic  0.86 us (2%)
  between operations  0.64 us (1%)
    pallas_call x1, Pallas kernels, shards(): pl.pallas_call(kernel, out_shape=vmem((2 * RANK, D), F32), in_specs=[hbm_...  54.8 us

profile of v6, /device:TPU:1, one launch (start us, length us, event | category | flops | bytes accessed | tf_op | source)
XLA Modules:
  0.0 56.3 jit_solution(9022350492196332162)
XLA Ops:
  0.6 54.8 %power_step.1 = f32[64,2304]{1,0:T(8,128)S(1)} custom-call(bf16[512,2304]{1,0:T(8,128)(2,1)} %hidden.1, bf16[288,512]{1,0:T(8,128)(2,1)} %bitcast.8, f32[288]{0:T(512)} %head.1, f32[1,16]{1,0:T(1,128)} %bitcast.11, s32[2,16]{1,0:T(2,128)} %bitcast.10, bf16[1,2304,2304]{2,1,0:T(8,128)(2,1)} %error.1, f32[32,2304]{1,0:T(8,128)} %bitcast.9), custom_call_target="tpu_custom_call" | custom-call | flops 2000000000 | bytes 14000000 | tf_op jit(solution)/shard_map/power_step/pallas_call | solution.py:406
  55.4 0.9 %multiply_bitcast_fusion = (f32[2304,32]{0,1:T(8,128)}, f32[2304,32]{0,1:T(8,128)}) fusion(f32[64,2304]{1,0:T(8,128)S(1)} %power_step.1), kind=kLoop, calls=%fused_computation | loop fusion | flops 147456 | bytes 1179648 | tf_op jit(solution)/shard_map/mul | solution.py:437
